TPU v7x, 32 devices: a whole 2x2x4 slice. The times are simulated.
32 devices in a mesh: wave: 16 (over z, y, x), lev: 2 (over core).
Axes of the slice: x: 2, y: 2, z: 4, core: 2. Of those that a mesh axis runs over, the one named last changes fastest.
Arguments:
- fourier_in: bfloat16 [3, 28, 1280, 64], P(None, 'lev', 'wave'), may hold values from -6 to 6
- spectral_old: bfloat16 [3, 28, 16, 2816], P(None, 'lev', 'wave'), may hold values from -6 to 6
- legendre: bfloat16 [16, 1408, 1280], P('wave'), may hold values from -0.15625 to 0.15625
- g_matrix: float32 [28, 28], replicated, may hold values from -1 to 1
- modes_in: float32 [28, 28], replicated, may hold values from -1 to 1
- modes_out: float32 [28, 28], replicated, may hold values from -1 to 1
- mode_heating: float32 [28, 28], replicated, may hold values from -1 to 1
- mode_rates: float32 [28], replicated, may hold values from 0.1 to 10
- pair_ids: int32 [16], replicated, may hold values from 0 to 639, as said below
- lat_ids: int32 [1280], replicated, may hold values from 0 to 1279, each once
- limits: int32 [1280], replicated, may hold values from 10 to 1280
Outputs:
- spectral_new: bfloat16 [3, 28, 16, 2816], P(None, 'lev', 'wave')
- fourier_out: bfloat16 [3, 28, 1280, 64], P(None, 'lev', 'wave')
Inputs may be any that keep to these rules, and one draw needn't show every extreme that they name: `pair_ids`: distinct pair numbers. `lat_ids`: each latitude once.
All inputs are finite; a program needn't handle non-finite values.
Results may differ from a plain program's by a relative error of at most 0.018.
Values may be sent and summed in bfloat16 or wider, within the bound.
A program may use at most 64 MiB of HBM per device.

v0:
```python
import jax
import jax.numpy as jnp
from jax import lax
from jax.sharding import PartitionSpec as P

MMAX = 1280
BLOCK = 64
coupling = 2.0
highest = lax.Precision.HIGHEST


def pair_layout(pair_number, row_count):
    row_index = jnp.arange(row_count, dtype=jnp.int32)
    first_length = MMAX - pair_number
    first_pad = (first_length + BLOCK - 1) // BLOCK * BLOCK
    in_first = row_index < first_pad
    row_valid = jnp.where(
        in_first, row_index < first_length, row_index - first_pad < pair_number + 1
    )
    degree = jnp.where(
        in_first, pair_number + row_index, MMAX - 1 - pair_number + row_index - first_pad
    ).astype(jnp.float32)
    lfactor = degree * (degree + 1.0) / float(MMAX * (MMAX - 1))
    return (row_valid, lfactor, first_pad)


def level_term(matrix, vector, level_start, lev_count, row_start, row_total):
    rows_block = lax.dynamic_slice(
        matrix, (jnp.asarray(row_start, jnp.int32), level_start), (row_total, lev_count)
    )
    return jnp.dot(rows_block, vector, precision=highest, preferred_element_type=jnp.float32)


def legendre_forward(stacked, pair_table, first_pad, pair_number, row_count):
    column_count = stacked.shape[1]

    def block_step(block_index, running, which_wave):
        start_row = block_index * BLOCK
        table_rows = lax.dynamic_slice_in_dim(pair_table, start_row, BLOCK, 0)
        product = lax.dot_general(
            stacked[which_wave],
            table_rows,
            (((1,), (1,)), ((), ())),
            preferred_element_type=jnp.float32,
        )
        return lax.dynamic_update_slice_in_dim(running, product, start_row, 1)

    running = jnp.zeros((column_count, row_count), jnp.float32)
    split_block = first_pad // BLOCK
    end_block = (first_pad + pair_number + BLOCK) // BLOCK
    running = lax.fori_loop(
        0, split_block, lambda block_index, carried: block_step(block_index, carried, 0), running
    )
    running = lax.fori_loop(
        split_block,
        end_block,
        lambda block_index, carried: block_step(block_index, carried, 1),
        running,
    )
    return running


def legendre_inverse(slot_spectra, pair_table, first_pad, pair_number):
    column_count = slot_spectra.shape[0]
    lat_total = pair_table.shape[1]

    def block_step(block_index, running):
        start_row = block_index * BLOCK
        table_rows = lax.dynamic_slice_in_dim(pair_table, start_row, BLOCK, 0)
        spectra_rows = lax.dynamic_slice_in_dim(slot_spectra, start_row, BLOCK, 1)
        return running + jnp.dot(spectra_rows, table_rows, preferred_element_type=jnp.float32)

    zeros_grid = jnp.zeros((column_count, lat_total), jnp.float32)
    split_block = first_pad // BLOCK
    end_block = (first_pad + pair_number + BLOCK) // BLOCK
    first_wave = lax.fori_loop(0, split_block, block_step, zeros_grid)
    second_wave = lax.fori_loop(split_block, end_block, block_step, zeros_grid)
    return jnp.stack([first_wave, second_wave])


def body(
    fourier_in,
    spectral_old,
    legendre,
    g_matrix,
    modes_in,
    modes_out,
    mode_heating,
    mode_rates,
    pair_ids,
    lat_ids,
    limits,
):
    lev_count = fourier_in.shape[1]
    lat_count = fourier_in.shape[2]
    pair_count = legendre.shape[0]
    row_count = legendre.shape[1]
    lat_total = legendre.shape[2]
    wave_index = lax.axis_index("wave")
    level_start = lax.axis_index("lev") * lev_count
    pair_slot = 0
    pair_number = lax.dynamic_slice_in_dim(pair_ids, wave_index * pair_count + pair_slot, 1)[0]
    layouts = [(pair_number,) + pair_layout(pair_number, row_count)]
    own_lats = lax.dynamic_slice_in_dim(lat_ids, wave_index * lat_count, lat_count)
    matches = own_lats[:, None] == jnp.arange(lat_total, dtype=jnp.int32)[None, :]
    row_limit = jnp.sum(jnp.where(matches, limits[None, :], 0), axis=1)
    both_waves = jnp.stack([pair_ids, MMAX - 1 - pair_ids], axis=1)
    column_wave = jnp.repeat(both_waves, 2, axis=1).reshape(-1)
    keep_mask = column_wave[None, :] < row_limit[:, None]
    masked = jnp.where(keep_mask[None, None], fourier_in, jnp.zeros((), fourier_in.dtype))
    exchanged = lax.all_to_all(masked, "wave", split_axis=3, concat_axis=2, tiled=True)
    item_count = exchanged.shape[0]
    column_count = item_count * lev_count * 2
    pair_slot = 0
    pair_number, row_valid, lfactor, first_pad = layouts[pair_slot]
    slot_data = exchanged.reshape(item_count, lev_count, lat_total, 2, 2)
    stacked = jnp.transpose(slot_data, (3, 0, 1, 4, 2)).reshape(2, column_count, lat_total)
    spectra = legendre_forward(stacked, legendre[pair_slot], first_pad, pair_number, row_count)
    spectra = jnp.where(row_valid[None, :], spectra, 0.0)
    results = [spectra.reshape(item_count, lev_count, 2, row_count)]
    tendency = jnp.stack(results, axis=2)
    flat_size = pair_count * 2 * row_count
    old_fields = spectral_old.reshape(3, lev_count, pair_count, 2, row_count).astype(jnp.float32)
    vorticity = (old_fields[0] + tendency[0]).reshape(lev_count, flat_size)
    divergence = (old_fields[1] + tendency[1]).reshape(lev_count, flat_size)
    heat_star = (old_fields[2] + tendency[2]).reshape(lev_count, flat_size)
    wave_factor = jnp.stack(
        [jnp.broadcast_to(layout[2][None, :], (2, row_count)) for layout in layouts]
    ).reshape(1, flat_size)
    keep_rows = jnp.stack(
        [jnp.broadcast_to(layout[1][None, :], (2, row_count)) for layout in layouts]
    ).reshape(1, flat_size)
    rates_own = lax.dynamic_slice_in_dim(mode_rates, level_start, lev_count)
    hydrostatic = lax.psum_scatter(
        level_term(
            g_matrix,
            heat_star,
            level_start,
            lev_count,
            jnp.int32(0),
            lev_count * lax.axis_size("lev"),
        ).astype(jnp.bfloat16),
        "lev",
        scatter_dimension=0,
        tiled=True,
    ).astype(jnp.float32)
    right_own = divergence + coupling * wave_factor * hydrostatic
    projected = lax.psum_scatter(
        level_term(
            modes_in,
            right_own,
            level_start,
            lev_count,
            jnp.int32(0),
            lev_count * lax.axis_size("lev"),
        ).astype(jnp.bfloat16),
        "lev",
        scatter_dimension=0,
        tiled=True,
    ).astype(jnp.float32)
    modal_part = projected / (1.0 + coupling * coupling * wave_factor * rates_own[:, None])
    row_start = jnp.int32(0)
    row_total = lev_count * lax.axis_size("lev")
    divergence_part = level_term(
        modes_out, modal_part, level_start, lev_count, row_start, row_total
    )
    heating_part = level_term(
        mode_heating, modal_part, level_start, lev_count, row_start, row_total
    )
    rebuilt = lax.psum_scatter(
        jnp.stack([divergence_part, heating_part], axis=1).astype(jnp.bfloat16),
        "lev",
        scatter_dimension=0,
        tiled=True,
    ).astype(jnp.float32)
    vorticity_out = jnp.where(keep_rows, vorticity, 0.0).astype(jnp.bfloat16)
    divergence_out = jnp.where(keep_rows, rebuilt[:, 0], 0.0).astype(jnp.bfloat16)
    heat_out = jnp.where(keep_rows, heat_star - coupling * rebuilt[:, 1], 0.0).astype(jnp.bfloat16)
    spectral_new = jnp.stack([vorticity_out, divergence_out, heat_out]).reshape(
        3, lev_count, pair_count, 2 * row_count
    )
    pair_slot = 0
    pair_number, row_valid, lfactor, first_pad = layouts[pair_slot]
    slot_spectra = spectral_new[:, :, pair_slot].reshape(3 * lev_count * 2, row_count)
    grid_part = legendre_inverse(slot_spectra, legendre[pair_slot], first_pad, pair_number)
    grid_part = (
        grid_part.reshape(2, 3, lev_count, 2, lat_total)
        .transpose(1, 2, 4, 0, 3)
        .reshape(3, lev_count, lat_total, 4)
    )
    gridded = grid_part.astype(jnp.bfloat16)
    returned = lax.all_to_all(gridded, "wave", split_axis=2, concat_axis=3, tiled=True)
    fourier_out = jnp.where(keep_mask[None, None], returned, jnp.zeros((), jnp.bfloat16))
    return (spectral_new, fourier_out)


def solution(mesh):
    placed = (
        P(None, "lev", "wave", None),
        P(None, "lev", "wave", None),
        P("wave", None, None),
        P(),
        P(),
        P(),
        P(),
        P(),
        P(),
        P(),
        P(),
    )
    return jax.shard_map(
        body,
        mesh=mesh,
        in_specs=placed,
        out_specs=(P(None, "lev", "wave", None), P(None, "lev", "wave", None)),
        check_vma=False,
    )
```

profile of v0, /device:TPU:0, one launch (start us, length us, event | category | flops | bytes accessed | tf_op | source)
XLA Modules:
  0.0 189.5 jit_solution(12464096708221175484)
XLA Ops:
  9.6 0.9 select_reduce_fusion
  10.6 1.2 broadcast_select_fusion.1
  11.8 1.3 copy.81
  13.1 8.3 %all-to-all-start = ((bf16[3,14,80,64]{2,1,0,3:T(8,128)(2,1)}), bf16[3,14,80,64]{2,1,0,3:T(8,128)(2,1)S(1)}, u32[]{:S(2)}, u32[]{:S(2)}) async-start(bf16[3,14,80,64]{2,1,0,3:T(8,128)(2,1)} %copy.81), calls=%async_computation | async-start | bytes 1572864 | tf_op jit(solution)/shard_map/all_to_all | solution.py:111
  25.5 15.7 %all-to-all-done = bf16[3,14,80,64]{2,1,0,3:T(8,128)(2,1)S(1)} async-done(((bf16[3,14,80,64]{2,1,0,3:T(8,128)(2,1)}), bf16[3,14,80,64]{2,1,0,3:T(8,128)(2,1)S(1)}, u32[]{:S(2)}, u32[]{:S(2)}) %all-to-all-start) | async-done | bytes 430112 | tf_op jit(solution)/shard_map/all_to_all | solution.py:111
  41.7 1.1 reshape.292
  43.2 19.2 %while.40 = (s32[]{:T(128)}, f32[84,1408]{0,1:T(8,128)S(1)}, s32[]{:T(128)}, bf16[1408,1280]{1,0:T(8,128)(2,1)}, bf16[2,84,1280]{2,1,0:T(8,128)(2,1)S(1)}, /*index=5*/s32[]{:T(128)}, s32[]{:T(128)}, s32[]{:T(128)}, s32[]{:T(128)}) while((s32[]{:T(128)}, f32[84,1408]{0,1:T(8,128)S(1)}, s32[]{:T(128)}, bf16[1408,1280]{1,0:T(8,128)(2,1)}, ...), condition=%wide.region_2.3_spmd, body=%wide.region_1.2_spmd.sunk | while | flops 13762566 | bytes 423051 | solution.py:51
  43.2 1.1 fusion.76
  44.3 1.1 fusion.76
  45.5 1.1 fusion.76
  46.6 1.1 fusion.76
  47.7 1.1 fusion.76
  48.9 1.1 fusion.76
  50.0 1.1 fusion.76
  51.1 1.1 fusion.76
  52.3 1.1 fusion.76
  53.4 1.1 fusion.76
  54.5 1.1 fusion.76
  55.7 1.1 fusion.76
  56.8 1.1 fusion.76
  57.9 1.1 fusion.76
  59.1 1.1 fusion.76
  60.2 1.1 fusion.76
  61.3 1.1 fusion.76
  62.4 4.5 %while.41 = (s32[]{:T(128)}, f32[84,1408]{0,1:T(8,128)S(1)}, s32[]{:T(128)}, bf16[1408,1280]{1,0:T(8,128)(2,1)}, bf16[2,84,1280]{2,1,0:T(8,128)(2,1)S(1)}, /*index=5*/s32[]{:T(128)}, s32[]{:T(128)}, s32[]{:T(128)}, s32[]{:T(128)}) while((s32[]{:T(128)}, f32[84,1408]{0,1:T(8,128)S(1)}, s32[]{:T(128)}, bf16[1408,1280]{1,0:T(8,128)(2,1)}, ...), condition=%wide.region_4.5_spmd, body=%wide.region_3.4_spmd.sunk | while | flops 13762566 | bytes 423051 | solution.py:54
  62.5 1.1 fusion.79
  63.6 1.1 fusion.79
  64.7 1.1 fusion.79
  65.9 1.1 fusion.79
  68.6 3.0 %fusion = bf16[16,2816]{1,0:T(8,128)(2,1)S(1)} fusion(bf16[28,2816]{1,0:T(8,128)(2,1)S(1)} %convolution_convert_fusion.3), kind=kCustom, calls=%all-reduce-scatter | all-reduce-scatter fusion | flops 90113 | bytes 248320
  71.6 2.3 %collective-permute-start = (bf16[2,2816]{1,0:T(2,128)(2,1)S(1)}, bf16[2,2816]{1,0:T(2,128)(2,1)S(1)}, u32[]{:S(2)}, u32[]{:S(2)}) collective-permute-start(bf16[2,2816]{1,0:T(2,128)(2,1)S(1)} %slice.52), channel_id=1, source_target_pairs={{0,1},{2,3},{4,5},{6,7},{8,9},{10,11},{12,13},{14,15},{16,17},{18,... | collective-permute-start | bytes 33800
  76.9 3.0 %fusion.1 = bf16[16,2816]{1,0:T(8,128)(2,1)S(1)} fusion(bf16[28,2816]{1,0:T(8,128)(2,1)S(1)} %convolution_convert_fusion.2), kind=kCustom, calls=%all-reduce-scatter.1 | all-reduce-scatter fusion | flops 90113 | bytes 248320
  80.0 2.3 %collective-permute-start.1 = (bf16[2,2816]{1,0:T(2,128)(2,1)S(1)}, bf16[2,2816]{1,0:T(2,128)(2,1)S(1)}, u32[]{:S(2)}, u32[]{:S(2)}) collective-permute-start(bf16[2,2816]{1,0:T(2,128)(2,1)S(1)} %slice.53), channel_id=1, source_target_pairs={{0,1},{2,3},{4,5},{6,7},{8,9},{10,11},{12,13},{14,15},{16,17},{18,... | collective-permute-start | bytes 33800
  84.4 1.0 copy.89
  86.6 16.7 %all-reduce.7.cloned.1.call-done = bf16[28,2,2816]{2,1,0:T(2,128)(2,1)} async-done(((bf16[28,2,2816]{2,1,0:T(2,128)(2,1)}), bf16[28,2,2816]{2,1,0:T(2,128)(2,1)}) %all-reduce.7.cloned.1.call-update) | async-done | bytes 315408
  103.3 1.0 constant_dynamic-slice_fusion
  105.4 4.9 %while.43 = (s32[]{:T(128)}, f32[84,1280]{1,0:T(8,128)S(1)}, s32[]{:T(128)}, bf16[84,1408]{1,0:T(8,128)(2,1)S(1)}, bf16[1408,1280]{1,0:T(8,128)(2,1)}, /*index=5*/s32[]{:T(128)}, s32[]{:T(128)}, s32[]{:T(128)}, s32[]{:T(128)}) while((s32[]{:T(128)}, f32[84,1280]{1,0:T(8,128)S(1)}, s32[]{:T(128)}, bf16[84,1408]{1,0:T(8,128)(2,1)S(1)}, ...), condition=%wide.region_11.12_spmd, body=%wide.region_10.11_spmd.sunk | while | flops 13870086 | bytes 1068171 | solution.py:77
  105.4 1.2 convolution_add_fusion.5
  106.6 1.2 convolution_add_fusion.5
  107.8 1.2 convolution_add_fusion.5
  109.1 1.2 convolution_add_fusion.5
  110.4 20.7 %while.42 = (s32[]{:T(128)}, f32[84,1280]{1,0:T(8,128)S(1)}, s32[]{:T(128)}, bf16[84,1408]{1,0:T(8,128)(2,1)S(1)}, bf16[1408,1280]{1,0:T(8,128)(2,1)}, /*index=5*/s32[]{:T(128)}, s32[]{:T(128)}, s32[]{:T(128)}, s32[]{:T(128)}) while((s32[]{:T(128)}, f32[84,1280]{1,0:T(8,128)S(1)}, s32[]{:T(128)}, bf16[84,1408]{1,0:T(8,128)(2,1)S(1)}, ...), condition=%wide.region_9.10_spmd, body=%wide.region_8.9_spmd.sunk | while | flops 13870086 | bytes 1068171 | solution.py:76
  110.5 1.2 convolution_add_fusion.4
  111.7 1.2 convolution_add_fusion.4
  112.9 1.2 convolution_add_fusion.4
  114.1 1.2 convolution_add_fusion.4
  115.3 1.2 convolution_add_fusion.4
  116.6 1.2 convolution_add_fusion.4
  117.8 1.2 convolution_add_fusion.4
  119.0 1.2 convolution_add_fusion.4
  120.2 1.2 convolution_add_fusion.4
  121.4 1.2 convolution_add_fusion.4
  122.6 1.2 convolution_add_fusion.4
  123.9 1.2 convolution_add_fusion.4
  125.1 1.2 convolution_add_fusion.4
  126.3 1.2 convolution_add_fusion.4
  127.5 1.2 convolution_add_fusion.4
  128.7 1.2 convolution_add_fusion.4
  129.9 1.2 convolution_add_fusion.4
  131.9 6.4 %copy.98 = bf16[3,14,1280,2,2]{1,4,3,0,2:T(2,128)(2,1)} copy(bf16[3,14,1280,2,2]{2,4,3,1,0:T(2,128)(2,1)S(1)} %maximum_bitcast_fusion) | data formatting | bytes 860160 | tf_op jit(solution)/shard_map/convert_element_type | solution.py:191
  138.3 6.7 %reshape.298 = bf16[16,2,6720]{2,1,0:T(2,128)(2,1)S(1)} reshape(bf16[1280,3,4,14]{3,2,1,0:T(4,128)(2,1)} %bitcast.96) | data formatting | bytes 860160
  145.0 20.5 %all_to_all.33 = bf16[16,2,6720]{2,1,0:T(2,128)(2,1)S(1)} all-to-all(bf16[16,2,6720]{2,1,0:T(2,128)(2,1)S(1)} %reshape.298), channel_id=1, replica_groups=mesh['wave'=16,'lev'=2] {'wave'}, dimensions={0} | all-to-all | bytes 860160 | tf_op jit(solution)/shard_map/all_to_all | solution.py:192
  165.5 10.5 %reshape.299 = bf16[1280,3,4,14]{3,2,1,0:T(4,128)(2,1)} reshape(bf16[16,2,6720]{2,1,0:T(2,128)(2,1)S(1)} %all_to_all.33) | data formatting | bytes 860160
  175.9 5.5 %copy.99 = bf16[3,14,16,80,4]{3,2,4,1,0:T(8,128)(2,1)S(1)} copy(bf16[3,14,16,80,4]{1,4,0,3,2:T(4,128)(2,1)} %bitcast.97) | data formatting | bytes 860160 | tf_op jit(solution)/shard_map/all_to_all | solution.py:192
  (75 shorter events, 13.6 us)
Async XLA Ops:
  7.2 60.9 %copy-start = (f32[28,28]{1,0:T(8,128)S(1)}, f32[28,28]{1,0:T(8,128)}, u32[]{:S(2)}) copy-start(f32[28,28]{1,0:T(8,128)} %param.22) | copy-start | bytes 9412
  7.2 14.3 %copy-start.4 = (s32[16]{0:T(128)S(1)}, s32[16]{0:T(128)}, u32[]{:S(2)}) copy-start(s32[16]{0:T(128)} %param.27) | copy-start | bytes 196
  7.2 18.2 %copy-start.1 = (bf16[3,14,1,2816]{3,1,2,0:T(8,128)(2,1)S(1)}, bf16[3,14,1,2816]{3,1,2,0:T(8,128)(2,1)}, u32[]{:S(2)}) copy-start(bf16[3,14,1,2816]{3,1,2,0:T(8,128)(2,1)} %param.20) | copy-start | bytes 709636
  13.1 28.1 %all-to-all-start = ((bf16[3,14,80,64]{2,1,0,3:T(8,128)(2,1)}), bf16[3,14,80,64]{2,1,0,3:T(8,128)(2,1)S(1)}, u32[]{:S(2)}, u32[]{:S(2)}) async-start(bf16[3,14,80,64]{2,1,0,3:T(8,128)(2,1)} %copy.81), calls=%async_computation | async-start | bytes 1572864 | tf_op jit(solution)/shard_map/all_to_all | solution.py:111
  21.5 81.9 %all-reduce.7.cloned.1.call-start = ((), (), s32[]{:S(2)}) async-start(), calls=%async_computation.2 | async-start | bytes 630784
  67.0 7.6 %copy-start.3 = (u32[32]{0:T(128)S(1)}, u32[32]{0:T(128)}, u32[]{:S(2)}) copy-start(u32[32]{0:T(128)} %constant.117) | copy-start | bytes 388
  67.2 9.2 %copy-start.2 = (f32[28,28]{1,0:T(8,128)S(1)}, f32[28,28]{1,0:T(8,128)}, u32[]{:S(2)}) copy-start(f32[28,28]{1,0:T(8,128)} %param.23) | copy-start | bytes 9412
  67.3 15.0 %copy-start.7 = (f32[28]{0:T(128)S(1)}, f32[28]{0:T(128)}, u32[]{:S(2)}) copy-start(f32[28]{0:T(128)} %param.26) | copy-start | bytes 340
  67.3 16.1 %copy-start.5 = (f32[28,28]{1,0:T(8,128)S(1)}, f32[28,28]{1,0:T(8,128)}, u32[]{:S(2)}) copy-start(f32[28,28]{1,0:T(8,128)} %param.25) | copy-start | bytes 9412
  67.7 16.1 %copy-start.6 = (f32[28,28]{1,0:T(8,128)S(1)}, f32[28,28]{1,0:T(8,128)}, u32[]{:S(2)}) copy-start(f32[28,28]{1,0:T(8,128)} %param.24) | copy-start | bytes 9412
  71.6 4.5 %collective-permute-start = (bf16[2,2816]{1,0:T(2,128)(2,1)S(1)}, bf16[2,2816]{1,0:T(2,128)(2,1)S(1)}, u32[]{:S(2)}, u32[]{:S(2)}) collective-permute-start(bf16[2,2816]{1,0:T(2,128)(2,1)S(1)} %slice.52), channel_id=1, source_target_pairs={{0,1},{2,3},{4,5},{6,7},{8,9},{10,11},{12,13},{14,15},{16,17},{18,... | collective-permute-start | bytes 33800
  80.0 3.1 %collective-permute-start.1 = (bf16[2,2816]{1,0:T(2,128)(2,1)S(1)}, bf16[2,2816]{1,0:T(2,128)(2,1)S(1)}, u32[]{:S(2)}, u32[]{:S(2)}) collective-permute-start(bf16[2,2816]{1,0:T(2,128)(2,1)S(1)} %slice.53), channel_id=1, source_target_pairs={{0,1},{2,3},{4,5},{6,7},{8,9},{10,11},{12,13},{14,15},{16,17},{18,... | collective-permute-start | bytes 33800
Sparse Core Ops, SparseCore 0:
  85.6 17.6 all-reduce.6
where the time goes:
time: 191 us; the launch traced here: 190 us
  matrix products  50.2 us (26%)
  local copies, waits for them, and re-layouts  39.6 us (21%)
  waiting for transfers between devices  33.2 us (17%)
  blocking collectives  26.5 us (14%)
  between operations  19.2 us (10%)
  starting transfers between devices  12.9 us (7%)
  other arithmetic  6.88 us (4%)
    dot_general x21, matrix products, block_step(): jnp.dot(spectra_rows, table_rows, preferred_element_type=jnp.float32)  25 us
    dot_general x21, matrix products, block_step(): lax.dot_general(stacked[which_wave], table_rows, (((1,), (1,)), ((), ()))...  23.2 us
    all_to_all x1, blocking collectives, body(): lax.all_to_all(gridded, 'wave', split_axis=2, concat_axis=3, tiled=True)  20.5 us
    unnamed x24, local copies, waits for them, and re-layouts  19.4 us
    unnamed x4, waiting for transfers between devices  17.5 us
    all_to_all x1, waiting for transfers between devices, body(): lax.all_to_all(masked, 'wave', split_axis=3, concat_axis=2, tiled=True)  15.7 us
    all_to_all x1, starting transfers between devices, body(): lax.all_to_all(masked, 'wave', split_axis=3, concat_axis=2, tiled=True)  8.3 us
    convert_element_type x1, local copies, waits for them, and re-layouts, body(): gridded = grid_part.astype(jnp.bfloat16)  6.42 us
  transfers between devices with their start and end apart: 4, of which 3 were waited for; matrix products, arithmetic and copies ran while one was open for 1% of the time, Pallas kernels for 0%

commit v1 on v0

--- a/solution.py
+++ b/solution.py
@@ -189,7 +189,10 @@
         .reshape(3, lev_count, lat_total, 4)
     )
     gridded = grid_part.astype(jnp.bfloat16)
-    returned = lax.all_to_all(gridded, "wave", split_axis=2, concat_axis=3, tiled=True)
+    returned = jnp.concatenate(
+        lax.all_to_all(jnp.stack(jnp.split(gridded, lax.axis_size("wave"), axis=2)), "wave", 0, 0),
+        axis=3,
+    )
     fourier_out = jnp.where(keep_mask[None, None], returned, jnp.zeros((), jnp.bfloat16))
     return (spectral_new, fourier_out)
 

time: 191 us -> 170 us (0.89)
  local copies, waits for them, and re-layouts: 39.6 us -> 12.4 us
  blocking collectives: 26.5 us -> 32.4 us
    unnamed x24 -> x34, local copies, waits for them, and re-layouts: 19.4 us -> 4.72 us
    convert_element_type x1, local copies, waits for them, and re-layouts: 6.42 us -> 0.17 us  [body(): gridded = grid_part.astype(jnp.bfloat16)]
    all_to_all x1, blocking collectives: 20.5 us -> 26.5 us  [body(): lax.all_to_all(jnp.stack(jnp.split(gridded, lax.axis_size('wave'), axis=2...]
    all_to_all x2 -> x0, local copies, waits for them, and re-layouts: 5.79 us -> none  [body(): lax.all_to_all(gridded, 'wave', split_axis=2, concat_axis=3, tiled=True)]
  transfers between devices with their start and end apart: 4 -> 4, of which waited for: 3 -> 3; matrix products, arithmetic and copies ran while one was open for 1% -> 3% of each run, Pallas kernels for 0% -> 0%
where the time goes in v1:
time: 170 us; the launch traced here: 168 us
  matrix products  50.2 us (30%)
  blocking collectives  32.4 us (19%)
  waiting for transfers between devices  31.6 us (19%)
  between operations  19.2 us (11%)
  starting transfers between devices  12.9 us (8%)
  local copies, waits for them, and re-layouts  12.4 us (7%)
  other arithmetic  8.29 us (5%)
    all_to_all x1, blocking collectives, body(): lax.all_to_all(jnp.stack(jnp.split(gridded, lax.axis_size('wave'), axis=2...  26.5 us
    dot_general x21, matrix products, block_step(): jnp.dot(spectra_rows, table_rows, preferred_element_type=jnp.float32)  25 us
    dot_general x21, matrix products, block_step(): lax.dot_general(stacked[which_wave], table_rows, (((1,), (1,)), ((), ()))...  23.2 us
    unnamed x4, waiting for transfers between devices  17.5 us
    all_to_all x1, waiting for transfers between devices, body(): lax.all_to_all(masked, 'wave', split_axis=3, concat_axis=2, tiled=True)  14.1 us
    all_to_all x1, starting transfers between devices, body(): lax.all_to_all(masked, 'wave', split_axis=3, concat_axis=2, tiled=True)  8.3 us
    unnamed x2, blocking collectives  5.99 us
    unnamed x34, local copies, waits for them, and re-layouts  4.72 us
  transfers between devices with their start and end apart: 4, of which 3 were waited for; matrix products, arithmetic and copies ran while one was open for 3% of the time, Pallas kernels for 0%

profile of v1, /device:TPU:0, one launch (start us, length us, event | category | flops | bytes accessed | tf_op | source)
XLA Modules:
  0.0 168.3 jit_solution(2551574165118036272)
XLA Ops:
  8.8 0.8 dynamic_slice.40
  9.6 0.9 select_reduce_fusion
  10.6 2.4 %copy_select_fusion = bf16[3,14,80,64]{2,1,0,3:T(8,128)(2,1)} fusion(bf16[3,14,80,64]{2,3,1,0:T(8,128)(2,1)} %param.19, pred[80,64]{0,1:T(8,128)(4,1)S(1)} %broadcast_compare_fusion), kind=kLoop, calls=%fused_computation.27 | loop fusion | flops 215040 | bytes 865280 | tf_op jit(solution)/shard_map/jit(_where)/select_n | solution.py:110
  13.0 8.3 %all-to-all-start = ((bf16[3,14,80,64]{2,1,0,3:T(8,128)(2,1)}), bf16[3,14,80,64]{2,1,0,3:T(8,128)(2,1)S(1)}, u32[]{:S(2)}, u32[]{:S(2)}) async-start(bf16[3,14,80,64]{2,1,0,3:T(8,128)(2,1)} %copy_select_fusion), calls=%async_computation | async-start | bytes 1572864 | tf_op jit(solution)/shard_map/all_to_all | solution.py:111
  21.4 1.2 dynamic_slice.39
  25.3 1.0 convert_element_type.68
  26.9 14.1 %all-to-all-done = bf16[3,14,80,64]{2,1,0,3:T(8,128)(2,1)S(1)} async-done(((bf16[3,14,80,64]{2,1,0,3:T(8,128)(2,1)}), bf16[3,14,80,64]{2,1,0,3:T(8,128)(2,1)S(1)}, u32[]{:S(2)}, u32[]{:S(2)}) %all-to-all-start) | async-done | bytes 430112 | tf_op jit(solution)/shard_map/all_to_all | solution.py:111
  41.5 1.1 reshape.298
  43.0 19.3 %while.40 = (s32[]{:T(128)}, f32[84,1408]{0,1:T(8,128)S(1)}, s32[]{:T(128)}, bf16[1408,1280]{1,0:T(8,128)(2,1)}, bf16[2,84,1280]{2,1,0:T(8,128)(2,1)S(1)}, /*index=5*/s32[]{:T(128)}, s32[]{:T(128)}, s32[]{:T(128)}, s32[]{:T(128)}) while((s32[]{:T(128)}, f32[84,1408]{0,1:T(8,128)S(1)}, s32[]{:T(128)}, bf16[1408,1280]{1,0:T(8,128)(2,1)}, ...), condition=%wide.region_2.3_spmd, body=%wide.region_1.2_spmd.sunk | while | flops 13762566 | bytes 423051 | solution.py:51
  43.1 1.1 fusion.92
  44.2 1.1 fusion.92
  45.3 1.1 fusion.92
  46.5 1.1 fusion.92
  47.6 1.1 fusion.92
  48.7 1.1 fusion.92
  49.9 1.1 fusion.92
  51.0 1.1 fusion.92
  52.1 1.1 fusion.92
  53.3 1.1 fusion.92
  54.4 1.1 fusion.92
  55.6 1.1 fusion.92
  56.7 1.1 fusion.92
  57.8 1.1 fusion.92
  59.0 1.1 fusion.92
  60.1 1.1 fusion.92
  61.2 1.1 fusion.92
  62.4 4.5 %while.41 = (s32[]{:T(128)}, f32[84,1408]{0,1:T(8,128)S(1)}, s32[]{:T(128)}, bf16[1408,1280]{1,0:T(8,128)(2,1)}, bf16[2,84,1280]{2,1,0:T(8,128)(2,1)S(1)}, /*index=5*/s32[]{:T(128)}, s32[]{:T(128)}, s32[]{:T(128)}, s32[]{:T(128)}) while((s32[]{:T(128)}, f32[84,1408]{0,1:T(8,128)S(1)}, s32[]{:T(128)}, bf16[1408,1280]{1,0:T(8,128)(2,1)}, ...), condition=%wide.region_4.5_spmd, body=%wide.region_3.4_spmd.sunk | while | flops 13762566 | bytes 423051 | solution.py:54
  62.4 1.1 fusion.95
  63.5 1.1 fusion.95
  64.6 1.1 fusion.95
  65.8 1.1 fusion.95
  68.5 3.0 %fusion = bf16[16,2816]{1,0:T(8,128)(2,1)S(1)} fusion(bf16[28,2816]{1,0:T(8,128)(2,1)S(1)} %convolution_convert_fusion.3), kind=kCustom, calls=%all-reduce-scatter | all-reduce-scatter fusion | flops 90113 | bytes 248320
  71.5 2.3 %collective-permute-start = (bf16[2,2816]{1,0:T(2,128)(2,1)S(1)}, bf16[2,2816]{1,0:T(2,128)(2,1)S(1)}, u32[]{:S(2)}, u32[]{:S(2)}) collective-permute-start(bf16[2,2816]{1,0:T(2,128)(2,1)S(1)} %slice.52), channel_id=1, source_target_pairs={{0,1},{2,3},{4,5},{6,7},{8,9},{10,11},{12,13},{14,15},{16,17},{18,... | collective-permute-start | bytes 33800
  76.9 3.0 %fusion.1 = bf16[16,2816]{1,0:T(8,128)(2,1)S(1)} fusion(bf16[28,2816]{1,0:T(8,128)(2,1)S(1)} %convolution_convert_fusion.2), kind=kCustom, calls=%all-reduce-scatter.1 | all-reduce-scatter fusion | flops 90113 | bytes 248320
  79.9 2.3 %collective-permute-start.1 = (bf16[2,2816]{1,0:T(2,128)(2,1)S(1)}, bf16[2,2816]{1,0:T(2,128)(2,1)S(1)}, u32[]{:S(2)}, u32[]{:S(2)}) collective-permute-start(bf16[2,2816]{1,0:T(2,128)(2,1)S(1)} %slice.53), channel_id=1, source_target_pairs={{0,1},{2,3},{4,5},{6,7},{8,9},{10,11},{12,13},{14,15},{16,17},{18,... | collective-permute-start | bytes 33800
  84.3 1.0 copy.87
  86.5 16.8 %all-reduce.7.cloned.1.call-done = bf16[28,2,2816]{2,1,0:T(2,128)(2,1)} async-done(((bf16[28,2,2816]{2,1,0:T(2,128)(2,1)}), bf16[28,2,2816]{2,1,0:T(2,128)(2,1)}) %all-reduce.7.cloned.1.call-update) | async-done | bytes 315408
  103.2 1.0 constant_dynamic-slice_fusion
  104.4 0.8 pad_maximum_fusion.1
  105.3 20.8 %while.42 = (s32[]{:T(128)}, f32[84,1280]{1,0:T(8,128)S(1)}, s32[]{:T(128)}, bf16[84,1408]{1,0:T(8,128)(2,1)S(1)}, bf16[1408,1280]{1,0:T(8,128)(2,1)}, /*index=5*/s32[]{:T(128)}, s32[]{:T(128)}, s32[]{:T(128)}, s32[]{:T(128)}) while((s32[]{:T(128)}, f32[84,1280]{1,0:T(8,128)S(1)}, s32[]{:T(128)}, bf16[84,1408]{1,0:T(8,128)(2,1)S(1)}, ...), condition=%wide.region_9.10_spmd, body=%wide.region_8.9_spmd.sunk | while | flops 13870086 | bytes 1068171 | solution.py:76
  105.3 1.2 convolution_add_fusion.4
  106.6 1.2 convolution_add_fusion.4
  107.8 1.2 convolution_add_fusion.4
  109.0 1.2 convolution_add_fusion.4
  110.2 1.2 convolution_add_fusion.4
  111.4 1.2 convolution_add_fusion.4
  112.7 1.2 convolution_add_fusion.4
  113.9 1.2 convolution_add_fusion.4
  115.1 1.2 convolution_add_fusion.4
  116.3 1.2 convolution_add_fusion.4
  117.5 1.2 convolution_add_fusion.4
  118.8 1.2 convolution_add_fusion.4
  120.0 1.2 convolution_add_fusion.4
  121.2 1.2 convolution_add_fusion.4
  122.4 1.2 convolution_add_fusion.4
  123.6 1.2 convolution_add_fusion.4
  124.9 1.2 convolution_add_fusion.4
  126.3 4.9 %while.43 = (s32[]{:T(128)}, f32[84,1280]{1,0:T(8,128)S(1)}, s32[]{:T(128)}, bf16[84,1408]{1,0:T(8,128)(2,1)S(1)}, bf16[1408,1280]{1,0:T(8,128)(2,1)}, /*index=5*/s32[]{:T(128)}, s32[]{:T(128)}, s32[]{:T(128)}, s32[]{:T(128)}) while((s32[]{:T(128)}, f32[84,1280]{1,0:T(8,128)S(1)}, s32[]{:T(128)}, bf16[84,1408]{1,0:T(8,128)(2,1)S(1)}, ...), condition=%wide.region_11.12_spmd, body=%wide.region_10.11_spmd.sunk | while | flops 13870086 | bytes 1068171 | solution.py:77
  126.3 1.2 convolution_add_fusion.5
  127.5 1.2 convolution_add_fusion.5
  128.7 1.2 convolution_add_fusion.5
  130.0 1.2 convolution_add_fusion.5
  133.7 26.5 %all_to_all.20 = bf16[16,3,14,80,4]{3,4,2,1,0:T(4,128)(2,1)S(1)} all-to-all(bf16[16,3,14,80,4]{3,4,2,1,0:T(4,128)(2,1)S(1)} %fusion.45), channel_id=1, replica_groups=mesh['wave'=16,'lev'=2] {'wave'}, dimensions={0} | all-to-all | bytes 860160 | tf_op jit(solution)/shard_map/all_to_all | solution.py:193
  160.4 1.0 copy.94
  (84 shorter events, 12.2 us)
Async XLA Ops:
  7.2 60.8 %copy-start = (f32[28,28]{1,0:T(8,128)S(1)}, f32[28,28]{1,0:T(8,128)}, u32[]{:S(2)}) copy-start(f32[28,28]{1,0:T(8,128)} %param.22) | copy-start | bytes 9412
  13.0 28.1 %all-to-all-start = ((bf16[3,14,80,64]{2,1,0,3:T(8,128)(2,1)}), bf16[3,14,80,64]{2,1,0,3:T(8,128)(2,1)S(1)}, u32[]{:S(2)}, u32[]{:S(2)}) async-start(bf16[3,14,80,64]{2,1,0,3:T(8,128)(2,1)} %copy_select_fusion), calls=%async_computation | async-start | bytes 1572864 | tf_op jit(solution)/shard_map/all_to_all | solution.py:111
  21.3 81.9 %all-reduce.7.cloned.1.call-start = ((), (), s32[]{:S(2)}) async-start(), calls=%async_computation.2 | async-start | bytes 630784
  67.2 7.3 %copy-start.2 = (u32[32]{0:T(128)S(1)}, u32[32]{0:T(128)}, u32[]{:S(2)}) copy-start(u32[32]{0:T(128)} %constant.117) | copy-start | bytes 388
  67.2 9.2 %copy-start.1 = (f32[28,28]{1,0:T(8,128)S(1)}, f32[28,28]{1,0:T(8,128)}, u32[]{:S(2)}) copy-start(f32[28,28]{1,0:T(8,128)} %param.23) | copy-start | bytes 9412
  67.2 15.0 %copy-start.5 = (f32[28]{0:T(128)S(1)}, f32[28]{0:T(128)}, u32[]{:S(2)}) copy-start(f32[28]{0:T(128)} %param.26) | copy-start | bytes 340
  67.2 16.0 %copy-start.3 = (f32[28,28]{1,0:T(8,128)S(1)}, f32[28,28]{1,0:T(8,128)}, u32[]{:S(2)}) copy-start(f32[28,28]{1,0:T(8,128)} %param.24) | copy-start | bytes 9412
  67.7 16.1 %copy-start.4 = (f32[28,28]{1,0:T(8,128)S(1)}, f32[28,28]{1,0:T(8,128)}, u32[]{:S(2)}) copy-start(f32[28,28]{1,0:T(8,128)} %param.25) | copy-start | bytes 9412
  71.5 4.6 %collective-permute-start = (bf16[2,2816]{1,0:T(2,128)(2,1)S(1)}, bf16[2,2816]{1,0:T(2,128)(2,1)S(1)}, u32[]{:S(2)}, u32[]{:S(2)}) collective-permute-start(bf16[2,2816]{1,0:T(2,128)(2,1)S(1)} %slice.52), channel_id=1, source_target_pairs={{0,1},{2,3},{4,5},{6,7},{8,9},{10,11},{12,13},{14,15},{16,17},{18,... | collective-permute-start | bytes 33800
  79.9 3.1 %collective-permute-start.1 = (bf16[2,2816]{1,0:T(2,128)(2,1)S(1)}, bf16[2,2816]{1,0:T(2,128)(2,1)S(1)}, u32[]{:S(2)}, u32[]{:S(2)}) collective-permute-start(bf16[2,2816]{1,0:T(2,128)(2,1)S(1)} %slice.53), channel_id=1, source_target_pairs={{0,1},{2,3},{4,5},{6,7},{8,9},{10,11},{12,13},{14,15},{16,17},{18,... | collective-permute-start | bytes 33800
Sparse Core Ops, SparseCore 0:
  85.5 17.6 all-reduce.6
